TPU v7x, 32 devices: a whole 2x2x4 slice. The times are simulated.
32 devices in a mesh: paths: 2 (over x), qa: 8 (over z, y), qb: 2 (over core).
Axes of the slice: x: 2, y: 2, z: 4, core: 2. Of those that a mesh axis runs over, the one named last changes fastest.
Arguments:
- state: float32 [2, 4194304], P(None, ('paths', 'qa', 'qb')), parts along dimension 1, may hold values from -6 to 6
- gate_terms: float32 [18, 2, 2, 128, 128], replicated, may hold values from -0.375 to 0.375
- path_bits: int32 [36], P('paths'), parts along dimension 0, may hold values from 0 to 1
Outputs:
- final_state: float32 [2, 4194304], P(None, ('paths', 'qa', 'qb')), parts along dimension 1
There are 2 independent parts, one for each index of `paths`. A program takes and returns all parts, laid end to end along the dimension named above; an argument that names none is the same for every part. Nothing has to cross between parts.
All inputs are finite; a program needn't handle non-finite values.
Results may differ from a plain program's by a relative error of at most 0.00013.
Values sent between devices are 32-bit elements; how exact they have to be, the bound alone decides.
No kernel may reach another device: no remote copies, remote signals or barrier semaphores. Data moves between devices by JAX's collectives and lax.ppermute only.
A program may use at most 64 MiB of HBM per device.

v0:
```python
import functools

import jax
import jax.numpy as jnp
from jax import lax
from jax.experimental import pallas as pl
from jax.experimental.layout import Layout, with_layout_constraint
from jax.experimental.pallas import tpu as pltpu
from jax.sharding import PartitionSpec as P

F32 = jnp.float32
BF16 = jnp.bfloat16
VMEM_LIMIT = 48 * 1024 * 1024
CHUNKS = 2


def window_offsets(span, gate_bits):
    return [0, span, gate_bits, span - 1, gate_bits + 1, span - 2]


def plan_gates(local_bits, gate_bits):
    outer = window_offsets(local_bits - gate_bits, gate_bits)
    inner = window_offsets(local_bits - gate_bits - 1, gate_bits)
    low, sections = [], []
    for number, offsets in enumerate((outer, inner, outer)):
        section = []
        for index, offset in enumerate(offsets):
            gate = 6 * number + index
            if offset == 0:
                low.append(gate)
            elif section and section[-1][0] == offset:
                section[-1][1].append(gate)
            else:
                section.append((offset, [gate]))
        sections.append(section)
    return low, sections


def exact_dot(a, b):
    return lax.dot_general(
        a, b, (((1,), (0,)), ((), ())), precision=lax.Precision.HIGHEST, preferred_element_type=F32
    )


def split(x):
    high = x.astype(BF16)
    return high, (x - high.astype(F32)).astype(BF16)


def bf_dot(a, b):
    return jnp.dot(a, b, preferred_element_type=F32)


def prepare_kernel(low, heads, tails, bits_ref, gates_ref, low_ref, heads_ref, tails_ref, held, sems):
    copies = []
    for gate in range(held.shape[0]):
        copy = pltpu.make_async_copy(gates_ref.at[gate, bits_ref[gate]], held.at[gate], sems.at[gate])
        copy.start()
        copies.append(copy)
    for copy in copies:
        copy.wait()

    def block(real, imag):
        return jnp.concatenate(
            [jnp.concatenate([real, -imag], axis=1), jnp.concatenate([imag, real], axis=1)], axis=0
        )

    def product(gates):
        real, imag = held[gates[0], 0], held[gates[0], 1]
        for gate in gates[1:]:
            column = exact_dot(block(held[gate, 0], held[gate, 1]), jnp.concatenate([real, imag], axis=0))
            half = column.shape[0] // 2
            real, imag = column[:half], column[half:]
        return real, imag

    for target, products in ((heads_ref, heads), (tails_ref, tails)):
        for slot, gates in enumerate(products):
            high, rest = split(jnp.concatenate(product(gates), axis=1))
            target[slot] = jnp.concatenate([high, rest], axis=0)
    real, imag = product(low)
    dim = real.shape[0]
    part = dim // CHUNKS
    whole = block(real.T, -imag.T)
    pieces = []
    for chunk in range(CHUNKS):
        pieces += [whole[chunk * part : (chunk + 1) * part], whole[dim + chunk * part : dim + (chunk + 1) * part]]
    low_ref[0], low_ref[1] = split(jnp.concatenate(pieces, axis=0))


def pack_kernel(chunk, x_ref, out_ref):
    rows, lanes = out_ref.shape
    half = lanes // 2
    step = min(rows, 256)
    for start in range(0, rows, step):
        real = x_ref[pl.ds(2 * start, step, stride=2), :]
        imag = x_ref[pl.ds(2 * start + 1, step, stride=2), :]
        left = lax.broadcasted_iota(jnp.int32, real.shape, 1) < half
        if chunk == 0:
            value = jnp.where(left, real, pltpu.roll(imag, half, 1))
        else:
            value = jnp.where(left, pltpu.roll(real, half, 1), imag)
        out_ref[pl.ds(start, step), :] = value


def apply_rows(weights, offset, lane_bits, source, target):
    dim = weights.shape[0] // 2
    rows, lanes = source.shape
    stride = 2 ** (offset - lane_bits)
    starts = [h * dim * stride + l for h in range(rows // (dim * stride)) for l in range(stride)]
    high_w = weights[:dim]
    for pair in range(0, len(starts), 2):
        group = starts[pair : pair + 2]
        plain, turned = [], []
        for start in group:
            x = source[pl.ds(start, dim, stride=stride), :]
            left = lax.broadcasted_iota(jnp.int32, x.shape, 1) < lanes // 2
            moved = pltpu.roll(x, lanes // 2, 1)
            plain.append(x)
            turned.append(jnp.where(left, -moved, moved))
        x = jnp.concatenate([jnp.concatenate(plain, axis=1), jnp.concatenate(turned, axis=1)], axis=0)
        high, rest = split(x)
        both = bf_dot(weights, high)
        y = bf_dot(high_w, rest) + both[dim:] + both[:dim]
        for place, start in enumerate(group):
            target[pl.ds(start, dim, stride=stride), :] = y[:, place * lanes : (place + 1) * lanes]


def run_gates(section, weights_ref, lane_bits, source, buffers, target):
    for index, (offset, _) in enumerate(section):
        into = target if index == len(section) - 1 else buffers[index % 2]
        apply_rows(weights_ref[index], offset, lane_bits, source, into)
        source = into


def blocks_of(view):
    dests, tops, mids, inner, _ = view
    for top in range(tops):
        for mid in range(mids):
            for dest in range(dests):
                yield dest, top, mid, ((top * mids + mid) * dests + dest) * inner


def head_kernel(section, lane_bits, x_ref, weights_ref, out_ref, one, two):
    run_gates(section, weights_ref, lane_bits, x_ref, (one, two), two)
    inner = out_ref.shape[3]
    for dest, top, mid, start in blocks_of(out_ref.shape):
        out_ref[dest, top, mid] = two[pl.ds(start, inner), :]


def tail_rows(section, lane_bits, x_ref, weights_ref, one, two, target):
    inner = x_ref.shape[3]
    for dest, top, mid, start in blocks_of(x_ref.shape):
        two[pl.ds(start, inner), :] = x_ref[dest, top, mid]
    run_gates(section, weights_ref, lane_bits, two, (one, two), target)


def tail_kernel(section, lane_bits, x_ref, weights_ref, out_ref, one, two):
    tail_rows(section, lane_bits, x_ref, weights_ref, one, two, out_ref)


def last_kernel(section, lane_bits, x_ref, weights_ref, low_ref, other_ref, out_ref, one, two, three):
    tail_rows(section, lane_bits, x_ref, weights_ref, one, two, three)
    rows, lanes = three.shape
    step = min(rows, 256)
    for start in range(0, rows, step):
        high, rest = split(jnp.concatenate([other_ref[pl.ds(start, step), :], three[pl.ds(start, step), :]], axis=1))
        y = bf_dot(rest, low_ref[0]) + bf_dot(high, low_ref[1]) + bf_dot(high, low_ref[0])
        out_ref[pl.ds(2 * start, step, stride=2), :] = y[:, :lanes]
        out_ref[pl.ds(2 * start + 1, step, stride=2), :] = y[:, lanes:]


def in_vmem(count):
    return [pl.BlockSpec(memory_space=pltpu.VMEM)] * count


def call(kernel, name, out_shapes, in_specs, scratch, matmuls, *operands):
    many = isinstance(out_shapes, tuple)
    return pl.pallas_call(
        kernel,
        out_shape=out_shapes,
        in_specs=in_specs,
        out_specs=tuple(in_vmem(len(out_shapes))) if many else in_vmem(1)[0],
        scratch_shapes=scratch,
        compiler_params=pltpu.CompilerParams(vmem_limit_bytes=VMEM_LIMIT),
        cost_estimate=pl.CostEstimate(
            flops=matmuls * 3 * 2 * 128 * 256 * 1024, bytes_accessed=4 * 2**20, transcendentals=0
        ),
        name=name,
    )(*operands)


def per_device(state, gate_terms, path_bits):
    amps_local = state.shape[1]
    local_bits = amps_local.bit_length() - 1
    dim = gate_terms.shape[-1]
    gate_bits = dim.bit_length() - 1
    lanes = dim
    lane_bits = gate_bits
    rows = amps_local // lanes
    qa = lax.axis_size("qa")
    qb = lax.axis_size("qb")
    low, sections = plan_gates(local_bits, gate_bits)
    head = sections[0]
    tail = sections[1] + sections[2]

    low_w, head_w, tail_w = call(
        functools.partial(prepare_kernel, low, [g for _, g in head], [g for _, g in tail]),
        "prepare_gates",
        (
            jax.ShapeDtypeStruct((2, 2 * dim, 2 * dim), BF16),
            jax.ShapeDtypeStruct((len(head), 2 * dim, 2 * dim), BF16),
            jax.ShapeDtypeStruct((len(tail), 2 * dim, 2 * dim), BF16),
        ),
        [pl.BlockSpec(memory_space=pltpu.SMEM), pl.BlockSpec(memory_space=pl.ANY)],
        [
            pltpu.VMEM((gate_terms.shape[0], 2, dim, dim), F32),
            pltpu.SemaphoreType.DMA((gate_terms.shape[0],)),
        ],
        4,
        path_bits,
        gate_terms,
    )

    state = with_layout_constraint(state.reshape(2, rows, lanes), Layout(major_to_minor=(1, 0, 2)))
    state = state.swapaxes(0, 1).reshape(2 * rows, lanes)
    inner = rows // (qa * qa)
    view = (qa, qb, qa // qb, inner, lanes)
    buffer = pltpu.VMEM((rows, lanes), F32)

    packed = []
    for chunk in range(CHUNKS):
        piece = call(
            functools.partial(pack_kernel, chunk),
            f"pack_{chunk}",
            jax.ShapeDtypeStruct((rows, lanes), F32),
            in_vmem(1),
            [],
            0,
            state,
        )
        packed.append(piece.reshape(qa, rows // qa, lanes))
    arrived = [lax.all_to_all(piece, "qa", split_axis=0, concat_axis=0, tiled=True) for piece in packed]
    halfway = []
    for chunk in range(CHUNKS):
        piece = call(
            functools.partial(head_kernel, head, lane_bits),
            f"first_section_{chunk}",
            jax.ShapeDtypeStruct(view, F32),
            in_vmem(2),
            [buffer] * 2,
            len(head),
            arrived[chunk].reshape(rows, lanes),
            head_w,
        )
        piece = lax.all_to_all(
            piece.reshape(qa * qb, rows // (qa * qb), lanes), ("qa", "qb"), split_axis=0, concat_axis=0, tiled=True
        )
        halfway.append(piece.reshape(view))
    done = call(
        functools.partial(tail_kernel, tail, lane_bits),
        "later_sections_0",
        jax.ShapeDtypeStruct((rows, lanes), F32),
        in_vmem(2),
        [buffer] * 2,
        len(tail),
        halfway[0],
        tail_w,
    )
    final = call(
        functools.partial(last_kernel, tail, lane_bits),
        "later_sections_1",
        jax.ShapeDtypeStruct((2 * rows, lanes), F32),
        in_vmem(4),
        [buffer] * 3,
        len(tail) + 2,
        halfway[1],
        tail_w,
        low_w,
        done,
    )
    return final.reshape(rows, 2, lanes).swapaxes(0, 1).reshape(2, amps_local)


def solution(mesh):
    return jax.shard_map(
        per_device,
        mesh=mesh,
        in_specs=(P(None, ("paths", "qa", "qb")), P(), P("paths")),
        out_specs=P(None, ("paths", "qa", "qb")),
        check_vma=False,
    )
```

profile of v0, /device:TPU:0, one launch (start us, length us, event | category | flops | bytes accessed | tf_op | source)
XLA Modules:
  0.0 83.8 jit_solution(8721672106162162145)
XLA Ops:
  0.0 0.0 copy-start.2
  0.0 0.0 copy-start
  0.0 1.2 %copy-done = f32[2,131072]{1,0:T(2,128)S(1)} copy-done((f32[2,131072]{1,0:T(2,128)S(1)}, f32[2,131072]{1,0:T(2,128)}, u32[]{:S(2)}) %copy-start) | copy-done | bytes 1048600
  1.2 1.0 %pack_0.1 = f32[1024,128]{1,0:T(8,128)} custom-call(f32[2048,128]{1,0:T(8,128)S(1)} %bitcast.18), custom_call_target="tpu_custom_call" | custom-call | bytes 4194304 | tf_op jit(solution)/shard_map/pack_0/pallas_call | solution.py:178
  2.2 7.3 %all-to-all-start.2 = ((f32[8,128,128]{2,1,0:T(8,128)}), f32[8,128,128]{2,1,0:T(8,128)S(1)}, u32[]{:S(2)}, u32[]{:S(2)}) async-start(f32[8,128,128]{2,1,0:T(8,128)} %bitcast.9), calls=%async_computation.2 | async-start | bytes 1048576 | tf_op jit(solution)/shard_map/all_to_all | solution.py:242
  9.5 0.0 copy-start.1
  9.5 1.2 %copy-done.1 = f32[2,131072]{1,0:T(2,128)S(1)} copy-done((f32[2,131072]{1,0:T(2,128)S(1)}, f32[2,131072]{1,0:T(2,128)}, u32[]{:S(2)}) %copy-start.1) | copy-done | bytes 1048600
  10.7 1.0 %pack_1.1 = f32[1024,128]{1,0:T(8,128)} custom-call(f32[2048,128]{1,0:T(8,128)S(1)} %bitcast.19), custom_call_target="tpu_custom_call" | custom-call | bytes 4194304 | tf_op jit(solution)/shard_map/pack_1/pallas_call | solution.py:178
  11.7 12.3 %all-to-all-done.2 = f32[8,128,128]{2,1,0:T(8,128)S(1)} async-done(((f32[8,128,128]{2,1,0:T(8,128)}), f32[8,128,128]{2,1,0:T(8,128)S(1)}, u32[]{:S(2)}, u32[]{:S(2)}) %all-to-all-start.2) | async-done | bytes 524320 | tf_op jit(solution)/shard_map/all_to_all | solution.py:242
  24.0 3.6 %all-to-all-start = ((f32[8,128,128]{2,1,0:T(8,128)}), f32[8,128,128]{2,1,0:T(8,128)S(1)}, u32[]{:S(2)}, u32[]{:S(2)}) async-start(f32[8,128,128]{2,1,0:T(8,128)} %bitcast.3), calls=%async_computation | async-start | bytes 1048576 | tf_op jit(solution)/shard_map/all_to_all | solution.py:242
  27.6 0.0 copy-done.2
  27.6 4.3 %prepare_gates.1 = (bf16[2,256,256]{2,1,0:T(8,128)(2,1)S(1)}, bf16[4,256,256]{2,1,0:T(8,128)(2,1)S(1)}, bf16[8,256,256]{2,1,0:T(8,128)(2,1)S(1)}) custom-call(s32[18]{0:T(128)S(1)} %copy-done.2, f32[18,2,2,128,128]{4,3,2,1,0:T(8,128)} %gates_ref.1), custom_call_target="tpu_custom_call" | custom-call | flops 805306368 | bytes 4194304 | tf_op jit(solution)/shard_map/prepare_gates/pallas_call | solution.py:178
  32.0 2.6 %first_section_0.1 = f32[8,2,4,16,128]{4,3,2,1,0:T(8,128)} custom-call(f32[1024,128]{1,0:T(8,128)S(1)} %bitcast.21, bf16[4,256,256]{2,1,0:T(8,128)(2,1)S(1)} %get-tuple-element.8.weights_ref), custom_call_target="tpu_custom_call" | custom-call | flops 805306368 | bytes 4194304 | tf_op jit(solution)/shard_map/first_section_0/pallas_call | solution.py:178
  34.5 7.8 %all-to-all-done = f32[8,128,128]{2,1,0:T(8,128)S(1)} async-done(((f32[8,128,128]{2,1,0:T(8,128)}), f32[8,128,128]{2,1,0:T(8,128)S(1)}, u32[]{:S(2)}, u32[]{:S(2)}) %all-to-all-start) | async-done | bytes 524320 | tf_op jit(solution)/shard_map/all_to_all | solution.py:242
  42.3 3.7 %all-to-all-start.3 = ((f32[16,64,128]{2,1,0:T(8,128)}), f32[16,64,128]{2,1,0:T(8,128)S(1)}, u32[]{:S(2)}, u32[]{:S(2)}) async-start(f32[16,64,128]{2,1,0:T(8,128)} %bitcast.11), calls=%async_computation.3 | async-start | bytes 1048576 | tf_op jit(solution)/shard_map/all_to_all | solution.py:255
  46.1 2.6 %first_section_1.1 = f32[8,2,4,16,128]{4,3,2,1,0:T(8,128)} custom-call(f32[1024,128]{1,0:T(8,128)S(1)} %bitcast.20, bf16[4,256,256]{2,1,0:T(8,128)(2,1)S(1)} %get-tuple-element.8.weights_ref), custom_call_target="tpu_custom_call" | custom-call | flops 805306368 | bytes 4194304 | tf_op jit(solution)/shard_map/first_section_1/pallas_call | solution.py:178
  48.6 11.9 %all-to-all-done.3 = f32[16,64,128]{2,1,0:T(8,128)S(1)} async-done(((f32[16,64,128]{2,1,0:T(8,128)}), f32[16,64,128]{2,1,0:T(8,128)S(1)}, u32[]{:S(2)}, u32[]{:S(2)}) %all-to-all-start.3) | async-done | bytes 524320 | tf_op jit(solution)/shard_map/all_to_all | solution.py:255
  60.5 4.1 %all-to-all-start.1 = ((f32[16,64,128]{2,1,0:T(8,128)}), f32[16,64,128]{2,1,0:T(8,128)S(1)}, u32[]{:S(2)}, u32[]{:S(2)}) async-start(f32[16,64,128]{2,1,0:T(8,128)} %bitcast.5), calls=%async_computation.1 | async-start | bytes 1048576 | tf_op jit(solution)/shard_map/all_to_all | solution.py:255
  64.6 3.3 %later_sections_0.1.other_ref = f32[1024,128]{1,0:T(8,128)S(1)} custom-call(f32[8,2,4,16,128]{4,3,2,1,0:T(8,128)S(1)} %bitcast.22, bf16[8,256,256]{2,1,0:T(8,128)(2,1)S(1)} %get-tuple-element.9.weights_ref), custom_call_target="tpu_custom_call" | custom-call | flops 1610612736 | bytes 4194304 | tf_op jit(solution)/shard_map/later_sections_0/pallas_call | solution.py:178
  67.9 11.2 %all-to-all-done.1 = f32[16,64,128]{2,1,0:T(8,128)S(1)} async-done(((f32[16,64,128]{2,1,0:T(8,128)}), f32[16,64,128]{2,1,0:T(8,128)S(1)}, u32[]{:S(2)}, u32[]{:S(2)}) %all-to-all-start.1) | async-done | bytes 524320 | tf_op jit(solution)/shard_map/all_to_all | solution.py:255
  79.1 4.7 %later_sections_1.1 = f32[2048,128]{1,0:T(8,128)} custom-call(f32[8,2,4,16,128]{4,3,2,1,0:T(8,128)S(1)} %bitcast.23, bf16[8,256,256]{2,1,0:T(8,128)(2,1)S(1)} %get-tuple-element.9.weights_ref, bf16[2,256,256]{2,1,0:T(8,128)(2,1)S(1)} %get-tuple-element.10.low_ref, f32[1024,128]{1,0:T(8,128)S(1)} %later_sections_0.1.other_ref), custom_call_target="tpu_custom_call" | custom-call | flops 2013265920 | bytes 4194304 | tf_op jit(solution)/shard_map/later_sections_1/pallas_call | solution.py:178
Async XLA Ops:
  0.0 27.6 %copy-start.2 = (s32[18]{0:T(128)S(1)}, s32[18]{0:T(128)}, u32[]{:S(2)}) copy-start(s32[18]{0:T(128)} %bits_ref.1) | copy-start | bytes 220
  0.0 1.2 %copy-start = (f32[2,131072]{1,0:T(2,128)S(1)}, f32[2,131072]{1,0:T(2,128)}, u32[]{:S(2)}) copy-start(f32[2,131072]{1,0:T(2,128)} %param.3) | copy-start | bytes 3145732
  2.2 21.8 %all-to-all-start.2 = ((f32[8,128,128]{2,1,0:T(8,128)}), f32[8,128,128]{2,1,0:T(8,128)S(1)}, u32[]{:S(2)}, u32[]{:S(2)}) async-start(f32[8,128,128]{2,1,0:T(8,128)} %bitcast.9), calls=%async_computation.2 | async-start | bytes 1048576 | tf_op jit(solution)/shard_map/all_to_all | solution.py:242
  9.5 1.2 %copy-start.1 = (f32[2,131072]{1,0:T(2,128)S(1)}, f32[2,131072]{1,0:T(2,128)}, u32[]{:S(2)}) copy-start(f32[2,131072]{1,0:T(2,128)} %param.3) | copy-start | bytes 3145732
  24.0 18.3 %all-to-all-start = ((f32[8,128,128]{2,1,0:T(8,128)}), f32[8,128,128]{2,1,0:T(8,128)S(1)}, u32[]{:S(2)}, u32[]{:S(2)}) async-start(f32[8,128,128]{2,1,0:T(8,128)} %bitcast.3), calls=%async_computation | async-start | bytes 1048576 | tf_op jit(solution)/shard_map/all_to_all | solution.py:242
  42.3 18.2 %all-to-all-start.3 = ((f32[16,64,128]{2,1,0:T(8,128)}), f32[16,64,128]{2,1,0:T(8,128)S(1)}, u32[]{:S(2)}, u32[]{:S(2)}) async-start(f32[16,64,128]{2,1,0:T(8,128)} %bitcast.11), calls=%async_computation.3 | async-start | bytes 1048576 | tf_op jit(solution)/shard_map/all_to_all | solution.py:255
  60.5 18.6 %all-to-all-start.1 = ((f32[16,64,128]{2,1,0:T(8,128)}), f32[16,64,128]{2,1,0:T(8,128)S(1)}, u32[]{:S(2)}, u32[]{:S(2)}) async-start(f32[16,64,128]{2,1,0:T(8,128)} %bitcast.5), calls=%async_computation.1 | async-start | bytes 1048576 | tf_op jit(solution)/shard_map/all_to_all | solution.py:255
where the time goes:
time: 84.4 us; the launch traced here: 83.8 us
  waiting for transfers between devices  43.2 us (51%)
  Pallas kernels  19.4 us (23%)
  starting transfers between devices  18.8 us (22%)
  local copies, waits for them, and re-layouts  2.46 us (3%)
    all_to_all x2, waiting for transfers between devices, per_device(): lax.all_to_all(piece.reshape(qa * qb, rows // (qa * qb), lanes), ('qa', '...  23.1 us
    all_to_all x2, waiting for transfers between devices, per_device(): lax.all_to_all(piece, 'qa', split_axis=0, concat_axis=0, tiled=True)  20 us
    pallas_call x7, Pallas kernels, call(): pl.pallas_call(kernel, out_shape=out_shapes, in_specs=in_specs, out_specs...  19.4 us
    all_to_all x2, starting transfers between devices, per_device(): lax.all_to_all(piece, 'qa', split_axis=0, concat_axis=0, tiled=True)  10.9 us
    all_to_all x2, starting transfers between devices, per_device(): lax.all_to_all(piece.reshape(qa * qb, rows // (qa * qb), lanes), ('qa', '...  7.84 us
    unnamed x6, local copies, waits for them, and re-layouts  2.46 us
  transfers between devices with their start and end apart: 4, of which 4 were waited for; matrix products, arithmetic and copies ran while one was open for 0% of the time, Pallas kernels for 16%

commit v1 on v0

--- a/solution.py
+++ b/solution.py
@@ -87,19 +87,19 @@
     low_ref[0], low_ref[1] = split(jnp.concatenate(pieces, axis=0))
 
 
-def pack_kernel(chunk, x_ref, out_ref):
-    rows, lanes = out_ref.shape
-    half = lanes // 2
-    step = min(rows, 256)
-    for start in range(0, rows, step):
-        real = x_ref[pl.ds(2 * start, step, stride=2), :]
-        imag = x_ref[pl.ds(2 * start + 1, step, stride=2), :]
+def pack_kernel(chunk, x_ref, *outs):
+    me = lax.axis_index("qa")
+    for distance, out_ref in enumerate(outs):
+        block = jnp.bitwise_xor(me, distance)
+        rows, lanes = out_ref.shape
+        half = lanes // 2
+        real = x_ref[block, pl.ds(0, rows, stride=2), :]
+        imag = x_ref[block, pl.ds(1, rows, stride=2), :]
         left = lax.broadcasted_iota(jnp.int32, real.shape, 1) < half
         if chunk == 0:
-            value = jnp.where(left, real, pltpu.roll(imag, half, 1))
+            out_ref[...] = jnp.where(left, real, pltpu.roll(imag, half, 1))
         else:
-            value = jnp.where(left, pltpu.roll(real, half, 1), imag)
-        out_ref[pl.ds(start, step), :] = value
+            out_ref[...] = jnp.where(left, pltpu.roll(real, half, 1), imag)
 
 
 def apply_rows(weights, offset, lane_bits, source, target):
@@ -132,34 +132,59 @@
         source = into
 
 
-def blocks_of(view):
-    dests, tops, mids, inner, _ = view
-    for top in range(tops):
-        for mid in range(mids):
-            for dest in range(dests):
-                yield dest, top, mid, ((top * mids + mid) * dests + dest) * inner
-
-
-def head_kernel(section, lane_bits, x_ref, weights_ref, out_ref, one, two):
-    run_gates(section, weights_ref, lane_bits, x_ref, (one, two), two)
-    inner = out_ref.shape[3]
-    for dest, top, mid, start in blocks_of(out_ref.shape):
-        out_ref[dest, top, mid] = two[pl.ds(start, inner), :]
-
-
-def tail_rows(section, lane_bits, x_ref, weights_ref, one, two, target):
-    inner = x_ref.shape[3]
-    for dest, top, mid, start in blocks_of(x_ref.shape):
-        two[pl.ds(start, inner), :] = x_ref[dest, top, mid]
+def head_kernel(section, lane_bits, *refs):
+    *blocks, weights_ref, keep_ref, send_ref, one, two = refs
+    me = lax.axis_index("qa")
+    size = blocks[0].shape[0]
+    for distance, block_ref in enumerate(blocks):
+        start = pl.multiple_of(jnp.bitwise_xor(me, distance) * size, size)
+        one[pl.ds(start, size), :] = block_ref[...]
+    run_gates(section, weights_ref, lane_bits, one, (two, one), two)
+    half = two.shape[0] // 2
+    core = lax.axis_index("qb")
+    mine = pl.multiple_of(core * half, half)
+    other = pl.multiple_of((1 - core) * half, half)
+    keep_ref[...] = two[pl.ds(mine, half), :]
+    send_ref[...] = two[pl.ds(other, half), :]
+
+
+def middle_kernel(section, first, lane_bits, keep_ref, came_ref, weights_ref, *refs):
+    *outs, one, two = refs
+    half = keep_ref.shape[0]
+    core = lax.axis_index("qb")
+    one[pl.ds(pl.multiple_of(core * half, half), half), :] = keep_ref[...]
+    one[pl.ds(pl.multiple_of((1 - core) * half, half), half), :] = came_ref[...]
+    run_gates(section, weights_ref.at[pl.ds(first, len(section))], lane_bits, one, (two, one), two)
+    me = lax.axis_index("qa")
+    count = len(outs)
+    for distance, out_ref in enumerate(outs):
+        dest = jnp.bitwise_xor(me, distance)
+        inner = out_ref.shape[1]
+        for outer in range(out_ref.shape[0]):
+            start = pl.multiple_of((outer * count + dest) * inner, inner)
+            out_ref[outer] = two[pl.ds(start, inner), :]
+
+
+def tail_rows(section, lane_bits, blocks, weights_ref, one, two, target):
+    me = lax.axis_index("qa")
+    count = len(blocks)
+    for distance, block_ref in enumerate(blocks):
+        source = jnp.bitwise_xor(me, distance)
+        inner = block_ref.shape[1]
+        for outer in range(block_ref.shape[0]):
+            start = pl.multiple_of((outer * count + source) * inner, inner)
+            two[pl.ds(start, inner), :] = block_ref[outer]
     run_gates(section, weights_ref, lane_bits, two, (one, two), target)
 
 
-def tail_kernel(section, lane_bits, x_ref, weights_ref, out_ref, one, two):
-    tail_rows(section, lane_bits, x_ref, weights_ref, one, two, out_ref)
-
-
-def last_kernel(section, lane_bits, x_ref, weights_ref, low_ref, other_ref, out_ref, one, two, three):
-    tail_rows(section, lane_bits, x_ref, weights_ref, one, two, three)
+def tail_kernel(section, lane_bits, *refs):
+    *blocks, weights_ref, out_ref, one, two = refs
+    tail_rows(section, lane_bits, blocks, weights_ref, one, two, out_ref)
+
+
+def last_kernel(section, lane_bits, *refs):
+    *blocks, weights_ref, low_ref, other_ref, out_ref, one, two, three = refs
+    tail_rows(section, lane_bits, blocks, weights_ref, one, two, three)
     rows, lanes = three.shape
     step = min(rows, 256)
     for start in range(0, rows, step):
@@ -222,58 +247,72 @@
     )
 
     state = with_layout_constraint(state.reshape(2, rows, lanes), Layout(major_to_minor=(1, 0, 2)))
-    state = state.swapaxes(0, 1).reshape(2 * rows, lanes)
+    state = state.swapaxes(0, 1).reshape(qa, 2 * rows // qa, lanes)
     inner = rows // (qa * qa)
-    view = (qa, qb, qa // qb, inner, lanes)
     buffer = pltpu.VMEM((rows, lanes), F32)
-
-    packed = []
+    reach = max(i for i, (offset, _) in enumerate(head) if offset + gate_bits == local_bits) + 1
+
+    def exchange(blocks):
+        came = list(blocks)
+        for distance in reversed(range(1, qa)):
+            came[distance] = lax.ppermute(blocks[distance], "qa", [(i, i ^ distance) for i in range(qa)])
+        return came
+
+    arrived = []
     for chunk in range(CHUNKS):
-        piece = call(
+        blocks = call(
             functools.partial(pack_kernel, chunk),
             f"pack_{chunk}",
-            jax.ShapeDtypeStruct((rows, lanes), F32),
+            (jax.ShapeDtypeStruct((rows // qa, lanes), F32),) * qa,
             in_vmem(1),
             [],
             0,
             state,
         )
-        packed.append(piece.reshape(qa, rows // qa, lanes))
-    arrived = [lax.all_to_all(piece, "qa", split_axis=0, concat_axis=0, tiled=True) for piece in packed]
+        arrived.append(exchange(blocks))
     halfway = []
     for chunk in range(CHUNKS):
-        piece = call(
-            functools.partial(head_kernel, head, lane_bits),
-            f"first_section_{chunk}",
-            jax.ShapeDtypeStruct(view, F32),
-            in_vmem(2),
+        keep, send = call(
+            functools.partial(head_kernel, head[:reach], lane_bits),
+            f"first_section_top_{chunk}",
+            (jax.ShapeDtypeStruct((rows // 2, lanes), F32),) * 2,
+            in_vmem(qa + 1),
             [buffer] * 2,
-            len(head),
-            arrived[chunk].reshape(rows, lanes),
+            reach,
+            *arrived[chunk],
             head_w,
         )
-        piece = lax.all_to_all(
-            piece.reshape(qa * qb, rows // (qa * qb), lanes), ("qa", "qb"), split_axis=0, concat_axis=0, tiled=True
+        came = lax.ppermute(send, "qb", [(i, 1 - i) for i in range(qb)])
+        blocks = call(
+            functools.partial(middle_kernel, head[reach:], reach, lane_bits),
+            f"first_section_rest_{chunk}",
+            (jax.ShapeDtypeStruct((qa, inner, lanes), F32),) * qa,
+            in_vmem(3),
+            [buffer] * 2,
+            len(head) - reach,
+            keep,
+            came,
+            head_w,
         )
-        halfway.append(piece.reshape(view))
+        halfway.append(exchange(blocks))
     done = call(
         functools.partial(tail_kernel, tail, lane_bits),
         "later_sections_0",
         jax.ShapeDtypeStruct((rows, lanes), F32),
-        in_vmem(2),
+        in_vmem(qa + 1),
         [buffer] * 2,
         len(tail),
-        halfway[0],
+        *halfway[0],
         tail_w,
     )
     final = call(
         functools.partial(last_kernel, tail, lane_bits),
         "later_sections_1",
         jax.ShapeDtypeStruct((2 * rows, lanes), F32),
-        in_vmem(4),
+        in_vmem(qa + 3),
         [buffer] * 3,
         len(tail) + 2,
-        halfway[1],
+        *halfway[1],
         tail_w,
         low_w,
         done,

time: 84.4 us -> 75 us (0.89)
  waiting for transfers between devices: 43.2 us -> 15.6 us
  starting transfers between devices: 18.8 us -> 40.6 us
  Pallas kernels: 19.4 us -> 16.6 us
    all_to_all x4 -> x0, waiting for transfers between devices: 43.2 us -> none  [the longest x2 23.1 us: per_device(): lax.all_to_all(piece.reshape(qa * qb, rows // (qa * qb), lanes), ('qa', '...]
    ppermute x0 -> x30, starting transfers between devices: none -> 40.6 us  [the longest x28 40 us: exchange(): lax.ppermute(blocks[distance], 'qa', [(i, i ^ distance) for i in range(qa)])]
    all_to_all x4 -> x0, starting transfers between devices: 18.8 us -> none  [the longest x2 10.9 us: per_device(): lax.all_to_all(piece, 'qa', split_axis=0, concat_axis=0, tiled=True)]
    ppermute x0 -> x30, waiting for transfers between devices: none -> 15.6 us  [the longest x28 15.3 us: exchange(): lax.ppermute(blocks[distance], 'qa', [(i, i ^ distance) for i in range(qa)])]
    pallas_call x7 -> x9, Pallas kernels: 19.4 us -> 16.6 us  [call(): pl.pallas_call(kernel, out_shape=out_shapes, in_specs=in_specs, out_specs...]
    unnamed x6 -> x4, local copies, waits for them, and re-layouts: 2.46 us -> 1.88 us
  transfers between devices with their start and end apart: 4 -> 30, of which waited for: 4 -> 6; matrix products, arithmetic and copies ran while one was open for 0% -> 0% of each run, Pallas kernels for 16% -> 16%
where the time goes in v1:
time: 75 us; the launch traced here: 74.8 us
  starting transfers between devices  40.6 us (54%)
  Pallas kernels  16.6 us (22%)
  waiting for transfers between devices  15.6 us (21%)
  local copies, waits for them, and re-layouts  1.88 us (3%)
    ppermute x28, starting transfers between devices, exchange(): lax.ppermute(blocks[distance], 'qa', [(i, i ^ distance) for i in range(qa)])  40 us
    pallas_call x9, Pallas kernels, call(): pl.pallas_call(kernel, out_shape=out_shapes, in_specs=in_specs, out_specs...  16.6 us
    ppermute x28, waiting for transfers between devices, exchange(): lax.ppermute(blocks[distance], 'qa', [(i, i ^ distance) for i in range(qa)])  15.3 us
    unnamed x4, local copies, waits for them, and re-layouts  1.88 us
  transfers between devices with their start and end apart: 30, of which 6 were waited for; matrix products, arithmetic and copies ran while one was open for 0% of the time, Pallas kernels for 16%

profile of v1, /device:TPU:0, one launch (start us, length us, event | category | flops | bytes accessed | tf_op | source)
XLA Modules:
  0.0 74.8 jit_solution(1429733109374581097)
XLA Ops:
  0.0 1.2 %copy-done = f32[2,131072]{1,0:T(2,128)S(1)} copy-done((f32[2,131072]{1,0:T(2,128)S(1)}, f32[2,131072]{1,0:T(2,128)}, u32[]{:S(2)}) %copy-start) | copy-done | bytes 1048600
  1.4 3.0 %collective-permute-start.15 = (f32[128,128]{1,0:T(8,128)S(1)}, f32[128,128]{1,0:T(8,128)S(1)}, u32[]{:S(2)}, u32[]{:S(2)}) collective-permute-start(f32[128,128]{1,0:T(8,128)S(1)} %get-tuple-element.66), channel_id=1, source_target_pairs={{0,2},{2,0},{4,6},{6,4},{8,10},{10,8},{12,14},{14,12},{1,3},{3,1},... | collective-permute-start | bytes 196616 | tf_op jit(solution)/shard_map/ppermute | solution.py:258
  4.5 1.6 %collective-permute-start.16 = (f32[128,128]{1,0:T(8,128)S(1)}, f32[128,128]{1,0:T(8,128)S(1)}, u32[]{:S(2)}, u32[]{:S(2)}) collective-permute-start(f32[128,128]{1,0:T(8,128)S(1)} %get-tuple-element.67), channel_id=1, source_target_pairs={{0,4},{2,6},{4,0},{6,2},{8,12},{10,14},{12,8},{14,10},{1,5},{3,7},... | collective-permute-start | bytes 196616 | tf_op jit(solution)/shard_map/ppermute | solution.py:258
  6.8 3.0 %collective-permute-start.2 = (f32[128,128]{1,0:T(8,128)S(1)}, f32[128,128]{1,0:T(8,128)S(1)}, u32[]{:S(2)}, u32[]{:S(2)}) collective-permute-start(f32[128,128]{1,0:T(8,128)S(1)} %get-tuple-element.47), channel_id=1, source_target_pairs={{0,6},{2,4},{4,2},{6,0},{8,14},{10,12},{12,10},{14,8},{1,7},{3,5},... | collective-permute-start | bytes 196616 | tf_op jit(solution)/shard_map/ppermute | solution.py:258
  9.8 2.6 %collective-permute-start.3 = (f32[128,128]{1,0:T(8,128)S(1)}, f32[128,128]{1,0:T(8,128)S(1)}, u32[]{:S(2)}, u32[]{:S(2)}) collective-permute-start(f32[128,128]{1,0:T(8,128)S(1)} %get-tuple-element.48), channel_id=1, source_target_pairs={{0,8},{2,10},{4,12},{6,14},{8,0},{10,2},{12,4},{14,6},{1,9},{3,11}... | collective-permute-start | bytes 196616 | tf_op jit(solution)/shard_map/ppermute | solution.py:258
  12.7 2.5 %collective-permute-start.5 = (f32[128,128]{1,0:T(8,128)S(1)}, f32[128,128]{1,0:T(8,128)S(1)}, u32[]{:S(2)}, u32[]{:S(2)}) collective-permute-start(f32[128,128]{1,0:T(8,128)S(1)} %get-tuple-element.50), channel_id=1, source_target_pairs={{0,12},{2,14},{4,8},{6,10},{8,4},{10,6},{12,0},{14,2},{1,13},{3,15... | collective-permute-start | bytes 196616 | tf_op jit(solution)/shard_map/ppermute | solution.py:258
  15.2 2.3 %collective-permute-start.6 = (f32[128,128]{1,0:T(8,128)S(1)}, f32[128,128]{1,0:T(8,128)S(1)}, u32[]{:S(2)}, u32[]{:S(2)}) collective-permute-start(f32[128,128]{1,0:T(8,128)S(1)} %get-tuple-element.51), channel_id=1, source_target_pairs={{0,14},{2,12},{4,10},{6,8},{8,6},{10,4},{12,2},{14,0},{1,15},{3,13... | collective-permute-start | bytes 196616 | tf_op jit(solution)/shard_map/ppermute | solution.py:258
  17.5 2.2 %collective-permute-done.3.refs_4_ = f32[128,128]{1,0:T(8,128)S(1)} collective-permute-done((f32[128,128]{1,0:T(8,128)S(1)}, f32[128,128]{1,0:T(8,128)S(1)}, u32[]{:S(2)}, u32[]{:S(2)}) %collective-permute-start.3) | collective-permute-done | bytes 65568 | tf_op jit(solution)/shard_map/ppermute | solution.py:258
  19.7 0.8 %collective-permute-start.18 = (f32[128,128]{1,0:T(8,128)S(1)}, f32[128,128]{1,0:T(8,128)S(1)}, u32[]{:S(2)}, u32[]{:S(2)}) collective-permute-start(f32[128,128]{1,0:T(8,128)S(1)} %get-tuple-element.69), channel_id=1, source_target_pairs={{0,8},{2,10},{4,12},{6,14},{8,0},{10,2},{12,4},{14,6},{1,9},{3,11}... | collective-permute-start | bytes 196616 | tf_op jit(solution)/shard_map/ppermute | solution.py:258
  20.5 3.1 %collective-permute-done.4.refs_5_ = f32[128,128]{1,0:T(8,128)S(1)} collective-permute-done((f32[128,128]{1,0:T(8,128)S(1)}, f32[128,128]{1,0:T(8,128)S(1)}, u32[]{:S(2)}, u32[]{:S(2)}) %collective-permute-start.4) | collective-permute-done | bytes 65568 | tf_op jit(solution)/shard_map/ppermute | solution.py:258
  23.6 2.0 %collective-permute-start.20 = (f32[128,128]{1,0:T(8,128)S(1)}, f32[128,128]{1,0:T(8,128)S(1)}, u32[]{:S(2)}, u32[]{:S(2)}) collective-permute-start(f32[128,128]{1,0:T(8,128)S(1)} %get-tuple-element.71), channel_id=1, source_target_pairs={{0,12},{2,14},{4,8},{6,10},{8,4},{10,6},{12,0},{14,2},{1,13},{3,15... | collective-permute-start | bytes 196616 | tf_op jit(solution)/shard_map/ppermute | solution.py:258
  25.6 3.2 %collective-permute-start.21 = (f32[128,128]{1,0:T(8,128)S(1)}, f32[128,128]{1,0:T(8,128)S(1)}, u32[]{:S(2)}, u32[]{:S(2)}) collective-permute-start(f32[128,128]{1,0:T(8,128)S(1)} %get-tuple-element.72), channel_id=1, source_target_pairs={{0,14},{2,12},{4,10},{6,8},{8,6},{10,4},{12,2},{14,0},{1,15},{3,13... | collective-permute-start | bytes 196616 | tf_op jit(solution)/shard_map/ppermute | solution.py:258
  28.8 0.7 copy-done.1
  29.5 4.3 %prepare_gates.1 = (bf16[2,256,256]{2,1,0:T(8,128)(2,1)S(1)}, bf16[4,256,256]{2,1,0:T(8,128)(2,1)S(1)}, bf16[8,256,256]{2,1,0:T(8,128)(2,1)S(1)}) custom-call(s32[18]{0:T(128)S(1)} %copy-done.1, f32[18,2,2,128,128]{4,3,2,1,0:T(8,128)} %gates_ref.1), custom_call_target="tpu_custom_call" | custom-call | flops 805306368 | bytes 4194304 | tf_op jit(solution)/shard_map/prepare_gates/pallas_call | solution.py:203
  33.8 0.6 first_section_top_1.1
  34.5 0.6 first_section_top_0.1
  36.0 1.3 %first_section_rest_1.1 = (f32[8,16,128]{2,1,0:T(8,128)S(1)}, f32[8,16,128]{2,1,0:T(8,128)S(1)}, f32[8,16,128]{2,1,0:T(8,128)S(1)}, f32[8,16,128]{2,1,0:T(8,128)...) custom-call(f32[512,128]{1,0:T(8,128)S(1)} %get-tuple-element.53.kee, ...), custom_call_target="tpu_custom_call" | custom-call | flops 603979776 | bytes 4194304 | tf_op jit(solution)/shard_map/first_section_rest_1/pallas_call | solution.py:203
  37.3 1.1 %collective-permute-start.8 = (f32[8,16,128]{2,1,0:T(8,128)S(1)}, f32[8,16,128]{2,1,0:T(8,128)S(1)}, u32[]{:S(2)}, u32[]{:S(2)}) collective-permute-start(f32[8,16,128]{2,1,0:T(8,128)S(1)} %get-tuple-element.56), channel_id=1, source_target_pairs={{0,2},{2,0},{4,6},{6,4},{8,10},{10,8},{12,14},{14,12},{1,3},{3,1},... | collective-permute-start | bytes 196616 | tf_op jit(solution)/shard_map/ppermute | solution.py:258
  38.4 2.9 %collective-permute-start.9 = (f32[8,16,128]{2,1,0:T(8,128)S(1)}, f32[8,16,128]{2,1,0:T(8,128)S(1)}, u32[]{:S(2)}, u32[]{:S(2)}) collective-permute-start(f32[8,16,128]{2,1,0:T(8,128)S(1)} %get-tuple-element.57), channel_id=1, source_target_pairs={{0,4},{2,6},{4,0},{6,2},{8,12},{10,14},{12,8},{14,10},{1,5},{3,7},... | collective-permute-start | bytes 196616 | tf_op jit(solution)/shard_map/ppermute | solution.py:258
  41.4 1.3 %first_section_rest_0.1 = (f32[8,16,128]{2,1,0:T(8,128)S(1)}, f32[8,16,128]{2,1,0:T(8,128)S(1)}, f32[8,16,128]{2,1,0:T(8,128)S(1)}, f32[8,16,128]{2,1,0:T(8,128)...) custom-call(f32[512,128]{1,0:T(8,128)S(1)} %get-tuple-element.73.kee, ...), custom_call_target="tpu_custom_call" | custom-call | flops 603979776 | bytes 4194304 | tf_op jit(solution)/shard_map/first_section_rest_0/pallas_call | solution.py:203
  42.7 1.9 %collective-permute-start.23 = (f32[8,16,128]{2,1,0:T(8,128)S(1)}, f32[8,16,128]{2,1,0:T(8,128)S(1)}, u32[]{:S(2)}, u32[]{:S(2)}) collective-permute-start(f32[8,16,128]{2,1,0:T(8,128)S(1)} %get-tuple-element.76), channel_id=1, source_target_pairs={{0,2},{2,0},{4,6},{6,4},{8,10},{10,8},{12,14},{14,12},{1,3},{3,1},... | collective-permute-start | bytes 196616 | tf_op jit(solution)/shard_map/ppermute | solution.py:258
  44.6 1.6 %collective-permute-start.25 = (f32[8,16,128]{2,1,0:T(8,128)S(1)}, f32[8,16,128]{2,1,0:T(8,128)S(1)}, u32[]{:S(2)}, u32[]{:S(2)}) collective-permute-start(f32[8,16,128]{2,1,0:T(8,128)S(1)} %get-tuple-element.78), channel_id=1, source_target_pairs={{0,6},{2,4},{4,2},{6,0},{8,14},{10,12},{12,10},{14,8},{1,7},{3,5},... | collective-permute-start | bytes 196616 | tf_op jit(solution)/shard_map/ppermute | solution.py:258
  46.7 3.8 %collective-permute-start.27 = (f32[8,16,128]{2,1,0:T(8,128)S(1)}, f32[8,16,128]{2,1,0:T(8,128)S(1)}, u32[]{:S(2)}, u32[]{:S(2)}) collective-permute-start(f32[8,16,128]{2,1,0:T(8,128)S(1)} %get-tuple-element.80), channel_id=1, source_target_pairs={{0,10},{2,8},{4,14},{6,12},{8,2},{10,0},{12,6},{14,4},{1,11},{3,9}... | collective-permute-start | bytes 196616 | tf_op jit(solution)/shard_map/ppermute | solution.py:258
  50.5 0.6 collective-permute-start.28
  51.1 2.8 %collective-permute-start.29 = (f32[8,16,128]{2,1,0:T(8,128)S(1)}, f32[8,16,128]{2,1,0:T(8,128)S(1)}, u32[]{:S(2)}, u32[]{:S(2)}) collective-permute-start(f32[8,16,128]{2,1,0:T(8,128)S(1)} %get-tuple-element.82), channel_id=1, source_target_pairs={{0,14},{2,12},{4,10},{6,8},{8,6},{10,4},{12,2},{14,0},{1,15},{3,13... | collective-permute-start | bytes 196616 | tf_op jit(solution)/shard_map/ppermute | solution.py:258
  53.9 1.3 %collective-permute-done.26.refs_4_ = f32[8,16,128]{2,1,0:T(8,128)S(1)} collective-permute-done((f32[8,16,128]{2,1,0:T(8,128)S(1)}, f32[8,16,128]{2,1,0:T(8,128)S(1)}, u32[]{:S(2)}, u32[]{:S(2)}) %collective-permute-start.26) | collective-permute-done | bytes 65568 | tf_op jit(solution)/shard_map/ppermute | solution.py:258
  55.3 1.1 %collective-permute-start.11 = (f32[8,16,128]{2,1,0:T(8,128)S(1)}, f32[8,16,128]{2,1,0:T(8,128)S(1)}, u32[]{:S(2)}, u32[]{:S(2)}) collective-permute-start(f32[8,16,128]{2,1,0:T(8,128)S(1)} %get-tuple-element.59), channel_id=1, source_target_pairs={{0,8},{2,10},{4,12},{6,14},{8,0},{10,2},{12,4},{14,6},{1,9},{3,11}... | collective-permute-start | bytes 196616 | tf_op jit(solution)/shard_map/ppermute | solution.py:258
  56.4 5.2 %collective-permute-done.27.refs_5_ = f32[8,16,128]{2,1,0:T(8,128)S(1)} collective-permute-done((f32[8,16,128]{2,1,0:T(8,128)S(1)}, f32[8,16,128]{2,1,0:T(8,128)S(1)}, u32[]{:S(2)}, u32[]{:S(2)}) %collective-permute-start.27) | collective-permute-done | bytes 65568 | tf_op jit(solution)/shard_map/ppermute | solution.py:258
  61.8 1.6 %collective-permute-start.14 = (f32[8,16,128]{2,1,0:T(8,128)S(1)}, f32[8,16,128]{2,1,0:T(8,128)S(1)}, u32[]{:S(2)}, u32[]{:S(2)}) collective-permute-start(f32[8,16,128]{2,1,0:T(8,128)S(1)} %get-tuple-element.62), channel_id=1, source_target_pairs={{0,14},{2,12},{4,10},{6,8},{8,6},{10,4},{12,2},{14,0},{1,15},{3,13... | collective-permute-start | bytes 196616 | tf_op jit(solution)/shard_map/ppermute | solution.py:258
  63.4 3.3 %later_sections_0.1.refs_10_ = f32[1024,128]{1,0:T(8,128)S(1)} custom-call(f32[8,16,128]{2,1,0:T(8,128)S(1)} %get-tuple-element.75.refs_0_, f32[8,16,128]{2,1,0:T(8,128)S(1)} %collective-permute-done.23.refs_1_, f32[8,16,128]{2,1,0:T(8,128)S(1)} %collective-permute-done.24.refs_2_, f32[8,16,128]{2,1,0:T(8,128)S(1)} %collective-permute-done.25.refs_3_, ...), custom_call_target="tpu_custom_call" | custom-call | flops 1610612736 | bytes 4194304 | tf_op jit(solution)/shard_map/later_sections_0/pallas_call | solution.py:203
  66.7 3.3 %collective-permute-done.12.refs_5_ = f32[8,16,128]{2,1,0:T(8,128)S(1)} collective-permute-done((f32[8,16,128]{2,1,0:T(8,128)S(1)}, f32[8,16,128]{2,1,0:T(8,128)S(1)}, u32[]{:S(2)}, u32[]{:S(2)}) %collective-permute-start.12) | collective-permute-done | bytes 65568 | tf_op jit(solution)/shard_map/ppermute | solution.py:258
  70.0 4.7 %later_sections_1.1 = f32[2048,128]{1,0:T(8,128)} custom-call(f32[8,16,128]{2,1,0:T(8,128)S(1)} %get-tuple-element.55.refs_0_, f32[8,16,128]{2,1,0:T(8,128)S(1)} %collective-permute-done.8.refs_1_, f32[8,16,128]{2,1,0:T(8,128)S(1)} %collective-permute-done.9.refs_2_, f32[8,16,128]{2,1,0:T(8,128)S(1)} %collective-permute-done.10.refs_3_, ...), custom_call_target="tpu_custom_call" | custom-call | flops 2013265920 | bytes 4194304 | tf_op jit(solution)/shard_map/later_sections_1/pallas_call | solution.py:203
  (41 shorter events, 2.9 us)
Async XLA Ops:
  0.0 1.2 %copy-start = (f32[2,131072]{1,0:T(2,128)S(1)}, f32[2,131072]{1,0:T(2,128)}, u32[]{:S(2)}) copy-start(f32[2,131072]{1,0:T(2,128)} %param.3) | copy-start | bytes 3145732
  1.4 8.4 %collective-permute-start.15 = (f32[128,128]{1,0:T(8,128)S(1)}, f32[128,128]{1,0:T(8,128)S(1)}, u32[]{:S(2)}, u32[]{:S(2)}) collective-permute-start(f32[128,128]{1,0:T(8,128)S(1)} %get-tuple-element.66), channel_id=1, source_target_pairs={{0,2},{2,0},{4,6},{6,4},{8,10},{10,8},{12,14},{14,12},{1,3},{3,1},... | collective-permute-start | bytes 196616 | tf_op jit(solution)/shard_map/ppermute | solution.py:258
  4.5 7.9 %collective-permute-start.16 = (f32[128,128]{1,0:T(8,128)S(1)}, f32[128,128]{1,0:T(8,128)S(1)}, u32[]{:S(2)}, u32[]{:S(2)}) collective-permute-start(f32[128,128]{1,0:T(8,128)S(1)} %get-tuple-element.67), channel_id=1, source_target_pairs={{0,4},{2,6},{4,0},{6,2},{8,12},{10,14},{12,8},{14,10},{1,5},{3,7},... | collective-permute-start | bytes 196616 | tf_op jit(solution)/shard_map/ppermute | solution.py:258
  6.3 6.4 %collective-permute-start = (f32[128,128]{1,0:T(8,128)S(1)}, f32[128,128]{1,0:T(8,128)S(1)}, u32[]{:S(2)}, u32[]{:S(2)}) collective-permute-start(f32[128,128]{1,0:T(8,128)S(1)} %get-tuple-element.45), channel_id=1, source_target_pairs={{0,2},{2,0},{4,6},{6,4},{8,10},{10,8},{12,14},{14,12},{1,3},{3,1},... | collective-permute-start | bytes 196616 | tf_op jit(solution)/shard_map/ppermute | solution.py:258
  6.8 8.3 %collective-permute-start.1 = (f32[128,128]{1,0:T(8,128)S(1)}, f32[128,128]{1,0:T(8,128)S(1)}, u32[]{:S(2)}, u32[]{:S(2)}) collective-permute-start(f32[128,128]{1,0:T(8,128)S(1)} %get-tuple-element.46), channel_id=1, source_target_pairs={{0,4},{2,6},{4,0},{6,2},{8,12},{10,14},{12,8},{14,10},{1,5},{3,7},... | collective-permute-start | bytes 196616 | tf_op jit(solution)/shard_map/ppermute | solution.py:258
  6.8 10.6 %collective-permute-start.2 = (f32[128,128]{1,0:T(8,128)S(1)}, f32[128,128]{1,0:T(8,128)S(1)}, u32[]{:S(2)}, u32[]{:S(2)}) collective-permute-start(f32[128,128]{1,0:T(8,128)S(1)} %get-tuple-element.47), channel_id=1, source_target_pairs={{0,6},{2,4},{4,2},{6,0},{8,14},{10,12},{12,10},{14,8},{1,7},{3,5},... | collective-permute-start | bytes 196616 | tf_op jit(solution)/shard_map/ppermute | solution.py:258
  9.8 9.9 %collective-permute-start.3 = (f32[128,128]{1,0:T(8,128)S(1)}, f32[128,128]{1,0:T(8,128)S(1)}, u32[]{:S(2)}, u32[]{:S(2)}) collective-permute-start(f32[128,128]{1,0:T(8,128)S(1)} %get-tuple-element.48), channel_id=1, source_target_pairs={{0,8},{2,10},{4,12},{6,14},{8,0},{10,2},{12,4},{14,6},{1,9},{3,11}... | collective-permute-start | bytes 196616 | tf_op jit(solution)/shard_map/ppermute | solution.py:258
  12.4 11.2 %collective-permute-start.4 = (f32[128,128]{1,0:T(8,128)S(1)}, f32[128,128]{1,0:T(8,128)S(1)}, u32[]{:S(2)}, u32[]{:S(2)}) collective-permute-start(f32[128,128]{1,0:T(8,128)S(1)} %get-tuple-element.49), channel_id=1, source_target_pairs={{0,10},{2,8},{4,14},{6,12},{8,2},{10,0},{12,6},{14,4},{1,11},{3,9}... | collective-permute-start | bytes 196616 | tf_op jit(solution)/shard_map/ppermute | solution.py:258
  12.7 10.9 %collective-permute-start.5 = (f32[128,128]{1,0:T(8,128)S(1)}, f32[128,128]{1,0:T(8,128)S(1)}, u32[]{:S(2)}, u32[]{:S(2)}) collective-permute-start(f32[128,128]{1,0:T(8,128)S(1)} %get-tuple-element.50), channel_id=1, source_target_pairs={{0,12},{2,14},{4,8},{6,10},{8,4},{10,6},{12,0},{14,2},{1,13},{3,15... | collective-permute-start | bytes 196616 | tf_op jit(solution)/shard_map/ppermute | solution.py:258
  15.2 10.4 %collective-permute-start.6 = (f32[128,128]{1,0:T(8,128)S(1)}, f32[128,128]{1,0:T(8,128)S(1)}, u32[]{:S(2)}, u32[]{:S(2)}) collective-permute-start(f32[128,128]{1,0:T(8,128)S(1)} %get-tuple-element.51), channel_id=1, source_target_pairs={{0,14},{2,12},{4,10},{6,8},{8,6},{10,4},{12,2},{14,0},{1,15},{3,13... | collective-permute-start | bytes 196616 | tf_op jit(solution)/shard_map/ppermute | solution.py:258
  17.5 16.9 %collective-permute-start.17 = (f32[128,128]{1,0:T(8,128)S(1)}, f32[128,128]{1,0:T(8,128)S(1)}, u32[]{:S(2)}, u32[]{:S(2)}) collective-permute-start(f32[128,128]{1,0:T(8,128)S(1)} %get-tuple-element.68), channel_id=1, source_target_pairs={{0,6},{2,4},{4,2},{6,0},{8,14},{10,12},{12,10},{14,8},{1,7},{3,5},... | collective-permute-start | bytes 196616 | tf_op jit(solution)/shard_map/ppermute | solution.py:258
  19.7 14.8 %collective-permute-start.18 = (f32[128,128]{1,0:T(8,128)S(1)}, f32[128,128]{1,0:T(8,128)S(1)}, u32[]{:S(2)}, u32[]{:S(2)}) collective-permute-start(f32[128,128]{1,0:T(8,128)S(1)} %get-tuple-element.69), channel_id=1, source_target_pairs={{0,8},{2,10},{4,12},{6,14},{8,0},{10,2},{12,4},{14,6},{1,9},{3,11}... | collective-permute-start | bytes 196616 | tf_op jit(solution)/shard_map/ppermute | solution.py:258
  23.6 10.9 %collective-permute-start.19 = (f32[128,128]{1,0:T(8,128)S(1)}, f32[128,128]{1,0:T(8,128)S(1)}, u32[]{:S(2)}, u32[]{:S(2)}) collective-permute-start(f32[128,128]{1,0:T(8,128)S(1)} %get-tuple-element.70), channel_id=1, source_target_pairs={{0,10},{2,8},{4,14},{6,12},{8,2},{10,0},{12,6},{14,4},{1,11},{3,9}... | collective-permute-start | bytes 196616 | tf_op jit(solution)/shard_map/ppermute | solution.py:258
  23.6 10.9 %collective-permute-start.20 = (f32[128,128]{1,0:T(8,128)S(1)}, f32[128,128]{1,0:T(8,128)S(1)}, u32[]{:S(2)}, u32[]{:S(2)}) collective-permute-start(f32[128,128]{1,0:T(8,128)S(1)} %get-tuple-element.71), channel_id=1, source_target_pairs={{0,12},{2,14},{4,8},{6,10},{8,4},{10,6},{12,0},{14,2},{1,13},{3,15... | collective-permute-start | bytes 196616 | tf_op jit(solution)/shard_map/ppermute | solution.py:258
  25.6 8.9 %collective-permute-start.21 = (f32[128,128]{1,0:T(8,128)S(1)}, f32[128,128]{1,0:T(8,128)S(1)}, u32[]{:S(2)}, u32[]{:S(2)}) collective-permute-start(f32[128,128]{1,0:T(8,128)S(1)} %get-tuple-element.72), channel_id=1, source_target_pairs={{0,14},{2,12},{4,10},{6,8},{8,6},{10,4},{12,2},{14,0},{1,15},{3,13... | collective-permute-start | bytes 196616 | tf_op jit(solution)/shard_map/ppermute | solution.py:258
  28.8 0.7 copy-start.1
  34.4 1.6 %collective-permute-start.7 = (f32[512,128]{1,0:T(8,128)S(1)}, f32[512,128]{1,0:T(8,128)S(1)}, u32[]{:S(2)}, u32[]{:S(2)}) collective-permute-start(f32[512,128]{1,0:T(8,128)S(1)} %get-tuple-element.54), channel_id=1, source_target_pairs={{0,1},{1,0},{2,3},{3,2},{4,5},{5,4},{6,7},{7,6},{8,9},{9,8},{10,11... | collective-permute-start | bytes 786440 | tf_op jit(solution)/shard_map/ppermute | solution.py:285
  35.1 6.3 %collective-permute-start.22 = (f32[512,128]{1,0:T(8,128)S(1)}, f32[512,128]{1,0:T(8,128)S(1)}, u32[]{:S(2)}, u32[]{:S(2)}) collective-permute-start(f32[512,128]{1,0:T(8,128)S(1)} %get-tuple-element.74), channel_id=1, source_target_pairs={{0,1},{1,0},{2,3},{3,2},{4,5},{5,4},{6,7},{7,6},{8,9},{9,8},{10,11... | collective-permute-start | bytes 786440 | tf_op jit(solution)/shard_map/ppermute | solution.py:285
  37.3 8.9 %collective-permute-start.8 = (f32[8,16,128]{2,1,0:T(8,128)S(1)}, f32[8,16,128]{2,1,0:T(8,128)S(1)}, u32[]{:S(2)}, u32[]{:S(2)}) collective-permute-start(f32[8,16,128]{2,1,0:T(8,128)S(1)} %get-tuple-element.56), channel_id=1, source_target_pairs={{0,2},{2,0},{4,6},{6,4},{8,10},{10,8},{12,14},{14,12},{1,3},{3,1},... | collective-permute-start | bytes 196616 | tf_op jit(solution)/shard_map/ppermute | solution.py:258
  38.4 8.3 %collective-permute-start.9 = (f32[8,16,128]{2,1,0:T(8,128)S(1)}, f32[8,16,128]{2,1,0:T(8,128)S(1)}, u32[]{:S(2)}, u32[]{:S(2)}) collective-permute-start(f32[8,16,128]{2,1,0:T(8,128)S(1)} %get-tuple-element.57), channel_id=1, source_target_pairs={{0,4},{2,6},{4,0},{6,2},{8,12},{10,14},{12,8},{14,10},{1,5},{3,7},... | collective-permute-start | bytes 196616 | tf_op jit(solution)/shard_map/ppermute | solution.py:258
  42.7 7.8 %collective-permute-start.23 = (f32[8,16,128]{2,1,0:T(8,128)S(1)}, f32[8,16,128]{2,1,0:T(8,128)S(1)}, u32[]{:S(2)}, u32[]{:S(2)}) collective-permute-start(f32[8,16,128]{2,1,0:T(8,128)S(1)} %get-tuple-element.76), channel_id=1, source_target_pairs={{0,2},{2,0},{4,6},{6,4},{8,10},{10,8},{12,14},{14,12},{1,3},{3,1},... | collective-permute-start | bytes 196616 | tf_op jit(solution)/shard_map/ppermute | solution.py:258
  44.6 6.5 %collective-permute-start.24 = (f32[8,16,128]{2,1,0:T(8,128)S(1)}, f32[8,16,128]{2,1,0:T(8,128)S(1)}, u32[]{:S(2)}, u32[]{:S(2)}) collective-permute-start(f32[8,16,128]{2,1,0:T(8,128)S(1)} %get-tuple-element.77), channel_id=1, source_target_pairs={{0,4},{2,6},{4,0},{6,2},{8,12},{10,14},{12,8},{14,10},{1,5},{3,7},... | collective-permute-start | bytes 196616 | tf_op jit(solution)/shard_map/ppermute | solution.py:258
  44.6 9.3 %collective-permute-start.25 = (f32[8,16,128]{2,1,0:T(8,128)S(1)}, f32[8,16,128]{2,1,0:T(8,128)S(1)}, u32[]{:S(2)}, u32[]{:S(2)}) collective-permute-start(f32[8,16,128]{2,1,0:T(8,128)S(1)} %get-tuple-element.78), channel_id=1, source_target_pairs={{0,6},{2,4},{4,2},{6,0},{8,14},{10,12},{12,10},{14,8},{1,7},{3,5},... | collective-permute-start | bytes 196616 | tf_op jit(solution)/shard_map/ppermute | solution.py:258
  46.3 9.0 %collective-permute-start.26 = (f32[8,16,128]{2,1,0:T(8,128)S(1)}, f32[8,16,128]{2,1,0:T(8,128)S(1)}, u32[]{:S(2)}, u32[]{:S(2)}) collective-permute-start(f32[8,16,128]{2,1,0:T(8,128)S(1)} %get-tuple-element.79), channel_id=1, source_target_pairs={{0,8},{2,10},{4,12},{6,14},{8,0},{10,2},{12,4},{14,6},{1,9},{3,11}... | collective-permute-start | bytes 196616 | tf_op jit(solution)/shard_map/ppermute | solution.py:258
  46.7 14.9 %collective-permute-start.27 = (f32[8,16,128]{2,1,0:T(8,128)S(1)}, f32[8,16,128]{2,1,0:T(8,128)S(1)}, u32[]{:S(2)}, u32[]{:S(2)}) collective-permute-start(f32[8,16,128]{2,1,0:T(8,128)S(1)} %get-tuple-element.80), channel_id=1, source_target_pairs={{0,10},{2,8},{4,14},{6,12},{8,2},{10,0},{12,6},{14,4},{1,11},{3,9}... | collective-permute-start | bytes 196616 | tf_op jit(solution)/shard_map/ppermute | solution.py:258
  50.5 11.1 %collective-permute-start.28 = (f32[8,16,128]{2,1,0:T(8,128)S(1)}, f32[8,16,128]{2,1,0:T(8,128)S(1)}, u32[]{:S(2)}, u32[]{:S(2)}) collective-permute-start(f32[8,16,128]{2,1,0:T(8,128)S(1)} %get-tuple-element.81), channel_id=1, source_target_pairs={{0,12},{2,14},{4,8},{6,10},{8,4},{10,6},{12,0},{14,2},{1,13},{3,15... | collective-permute-start | bytes 196616 | tf_op jit(solution)/shard_map/ppermute | solution.py:258
  51.1 10.7 %collective-permute-start.29 = (f32[8,16,128]{2,1,0:T(8,128)S(1)}, f32[8,16,128]{2,1,0:T(8,128)S(1)}, u32[]{:S(2)}, u32[]{:S(2)}) collective-permute-start(f32[8,16,128]{2,1,0:T(8,128)S(1)} %get-tuple-element.82), channel_id=1, source_target_pairs={{0,14},{2,12},{4,10},{6,8},{8,6},{10,4},{12,2},{14,0},{1,15},{3,13... | collective-permute-start | bytes 196616 | tf_op jit(solution)/shard_map/ppermute | solution.py:258
  53.9 12.7 %collective-permute-start.10 = (f32[8,16,128]{2,1,0:T(8,128)S(1)}, f32[8,16,128]{2,1,0:T(8,128)S(1)}, u32[]{:S(2)}, u32[]{:S(2)}) collective-permute-start(f32[8,16,128]{2,1,0:T(8,128)S(1)} %get-tuple-element.58), channel_id=1, source_target_pairs={{0,6},{2,4},{4,2},{6,0},{8,14},{10,12},{12,10},{14,8},{1,7},{3,5},... | collective-permute-start | bytes 196616 | tf_op jit(solution)/shard_map/ppermute | solution.py:258
  55.3 11.4 %collective-permute-start.11 = (f32[8,16,128]{2,1,0:T(8,128)S(1)}, f32[8,16,128]{2,1,0:T(8,128)S(1)}, u32[]{:S(2)}, u32[]{:S(2)}) collective-permute-start(f32[8,16,128]{2,1,0:T(8,128)S(1)} %get-tuple-element.59), channel_id=1, source_target_pairs={{0,8},{2,10},{4,12},{6,14},{8,0},{10,2},{12,4},{14,6},{1,9},{3,11}... | collective-permute-start | bytes 196616 | tf_op jit(solution)/shard_map/ppermute | solution.py:258
  61.6 8.4 %collective-permute-start.12 = (f32[8,16,128]{2,1,0:T(8,128)S(1)}, f32[8,16,128]{2,1,0:T(8,128)S(1)}, u32[]{:S(2)}, u32[]{:S(2)}) collective-permute-start(f32[8,16,128]{2,1,0:T(8,128)S(1)} %get-tuple-element.60), channel_id=1, source_target_pairs={{0,10},{2,8},{4,14},{6,12},{8,2},{10,0},{12,6},{14,4},{1,11},{3,9}... | collective-permute-start | bytes 196616 | tf_op jit(solution)/shard_map/ppermute | solution.py:258
  61.6 8.4 %collective-permute-start.13 = (f32[8,16,128]{2,1,0:T(8,128)S(1)}, f32[8,16,128]{2,1,0:T(8,128)S(1)}, u32[]{:S(2)}, u32[]{:S(2)}) collective-permute-start(f32[8,16,128]{2,1,0:T(8,128)S(1)} %get-tuple-element.61), channel_id=1, source_target_pairs={{0,12},{2,14},{4,8},{6,10},{8,4},{10,6},{12,0},{14,2},{1,13},{3,15... | collective-permute-start | bytes 196616 | tf_op jit(solution)/shard_map/ppermute | solution.py:258
  61.8 8.3 %collective-permute-start.14 = (f32[8,16,128]{2,1,0:T(8,128)S(1)}, f32[8,16,128]{2,1,0:T(8,128)S(1)}, u32[]{:S(2)}, u32[]{:S(2)}) collective-permute-start(f32[8,16,128]{2,1,0:T(8,128)S(1)} %get-tuple-element.62), channel_id=1, source_target_pairs={{0,14},{2,12},{4,10},{6,8},{8,6},{10,4},{12,2},{14,0},{1,15},{3,13... | collective-permute-start | bytes 196616 | tf_op jit(solution)/shard_map/ppermute | solution.py:258
